TPU v7x, 128 devices: a whole 4x4x4 slice. The times are simulated.
128 devices in a mesh: frame: 8 (over z_lo, x), row: 16 (over z_hi, y, core).
Axes of the slice: x: 4, y: 4, z: 4 (z_hi: 2, z_lo: 2; z = z_hi * 2 + z_lo), core: 2. Of those that a mesh axis runs over, the one named last changes fastest.
Arguments:
- base_latent: bfloat16 [8, 64, 8, 3072], P(None, 'row', 'frame'), may hold values from -6 to 6
- degraded: bfloat16 [8, 128, 16, 3072], P('frame', 'row'), may hold values from -6 to 6
- row_window: int32 [128], replicated, may hold values from 0 to 23, as said below
- column_shift: int32 [1], replicated, may hold values from 0 to 7
- norm_gain: float32 [3072], replicated, may hold values from 0.1 to 1.9
- project_in: bfloat16 [3072, 3, 3072], P(None, None, 'frame'), may hold values from -4 to 4
- project_out: bfloat16 [3072, 3072], P('frame'), may hold values from -1.75 to 1.75
Outputs:
- restored: bfloat16 [8, 128, 16, 3072], P('frame', 'row')
Inputs may be any that keep to these rules, and one draw needn't show every extreme that they name: `row_window`: window numbers start at 0 and rise by one from a window to the next along the rows; each window has 1 to 8 rows, some have exactly 8, and there are 24 windows.
All inputs are finite; a program needn't handle non-finite values.
Results may differ from a plain program's by a relative error of at most 0.023.
Values may be sent and summed in bfloat16 or wider, within the bound.
A program may use at most 128 MiB of HBM per device.

v0:
```python
import jax
import jax.numpy as jnp
from jax import lax
from jax.sharding import PartitionSpec as P

HEAD = 128
ROWS_DEV = 8
WIN_COLS = 8


def extended(block, sides, width):
    for axis, dim in sides:
        count = lax.axis_size(axis)
        forward = [(i, i + 1) for i in range(count - 1)]
        backward = [(target, source) for source, target in forward]
        low = lax.ppermute(
            lax.slice_in_dim(block, block.shape[dim] - width, None, axis=dim), axis, forward
        )
        high = lax.ppermute(lax.slice_in_dim(block, 0, width, axis=dim), axis, backward)
        block = jnp.concatenate([low, block, high], axis=dim)
    return block


def rms_normed(values, norm_gain):
    widened = values.astype(jnp.float32)
    scale = lax.rsqrt(jnp.mean(widened * widened, axis=-1, keepdims=True) + 1e-06)
    return (widened * scale * norm_gain).astype(jnp.bfloat16)


def window_attention(query, keyval, query_ids, key_ids, offset):
    frame_count, row_count, column_count, feature_width = query.shape
    head_count = feature_width // HEAD
    windows = column_count // WIN_COLS
    key_rows = keyval.shape[1]
    query = jnp.roll(query, -offset, axis=2)
    keyval = jnp.roll(keyval, -offset, axis=2)
    query_blocks = query.reshape(frame_count, row_count, windows, WIN_COLS, head_count, HEAD)
    query_blocks = query_blocks.transpose(2, 4, 0, 1, 3, 5).reshape(
        windows * head_count, frame_count * row_count * WIN_COLS, HEAD
    )
    pair_blocks = keyval.reshape(frame_count, key_rows, windows, WIN_COLS, 2, head_count, HEAD)
    pair_blocks = pair_blocks.transpose(4, 2, 5, 0, 1, 3, 6).reshape(
        2, windows * head_count, frame_count * key_rows * WIN_COLS, HEAD
    )
    query_tokens = jnp.broadcast_to(
        query_ids[None, :, None], (frame_count, row_count, WIN_COLS)
    ).reshape(-1)
    key_tokens = jnp.broadcast_to(
        key_ids[None, :, None], (frame_count, key_rows, WIN_COLS)
    ).reshape(-1)
    allowed = (query_tokens[:, None] == key_tokens[None, :]) & (key_tokens[None, :] >= 0)

    def one_block(block_parts):
        query_block, key_block, value_block = block_parts
        scores = jnp.dot(query_block, key_block.T, preferred_element_type=jnp.float32) * HEAD ** (
            -0.5
        )
        scores = jnp.where(allowed, scores, -1e30)
        highest = jnp.max(scores, axis=-1, keepdims=True)
        raised = jnp.exp(scores - highest)
        weights = (raised / jnp.sum(raised, axis=-1, keepdims=True)).astype(jnp.bfloat16)
        return jnp.dot(weights, value_block, preferred_element_type=jnp.float32).astype(
            jnp.bfloat16
        )

    results = lax.map(one_block, (query_blocks, pair_blocks[0], pair_blocks[1]))
    results = results.reshape(windows, head_count, frame_count, row_count, WIN_COLS, HEAD)
    results = results.transpose(2, 3, 0, 4, 1, 5).reshape(
        frame_count, row_count, column_count, feature_width
    )
    return jnp.roll(results, offset, axis=2)


def local(base_latent, degraded, row_window, column_shift, norm_gain, project_in, project_out):
    fine_tokens = jnp.repeat(jnp.repeat(base_latent, 2, axis=1), 2, axis=2)
    upsampled = lax.all_to_all(fine_tokens, "frame", split_axis=0, concat_axis=2, tiled=True)
    mixed_tokens = (upsampled.astype(jnp.float32) + degraded.astype(jnp.float32)).astype(
        jnp.bfloat16
    )
    normed = rms_normed(mixed_tokens, norm_gain)
    row_count = normed.shape[1]
    column_count = normed.shape[2]
    local_width = project_in.shape[2]
    rim_tokens = extended(normed, (("row", 1),), ROWS_DEV)
    query_weight = project_in[:, 0]
    pair_weight = project_in[:, 1:]
    piece = lax.all_gather(rim_tokens, "frame", axis=0, tiled=True)
    frames_here = piece.shape[0]
    middle = piece[:, ROWS_DEV : 2 * ROWS_DEV]
    query_part = jnp.einsum(
        "frcd,dh->frch", middle, query_weight, preferred_element_type=jnp.float32
    ).astype(jnp.bfloat16)
    pair_part = jnp.einsum(
        "frcd,dkh->frckh", piece, pair_weight, preferred_element_type=jnp.float32
    ).astype(jnp.bfloat16)
    projected = jnp.concatenate(
        [
            query_part.reshape(frames_here, -1, local_width),
            pair_part.reshape(frames_here, -1, local_width),
        ],
        axis=1,
    )
    frame_total = projected.shape[0]
    query_length = row_count * column_count
    query = projected[:, :query_length].reshape(frame_total, row_count, column_count, local_width)
    keyval = projected[:, query_length:].reshape(
        frame_total, 3 * row_count, column_count, 2, local_width
    )
    first_row = lax.axis_index("row") * ROWS_DEV
    padded_ids = jnp.pad(row_window, (ROWS_DEV, ROWS_DEV), constant_values=-1)
    query_ids = lax.dynamic_slice_in_dim(padded_ids, first_row + ROWS_DEV, ROWS_DEV, 0)
    key_ids = lax.dynamic_slice_in_dim(padded_ids, first_row, 3 * ROWS_DEV, 0)
    attended = window_attention(query, keyval, query_ids, key_ids, column_shift[0])
    summed = lax.psum_scatter(
        jnp.einsum(
            "frck,ke->frce", attended, project_out, preferred_element_type=jnp.float32
        ).astype(jnp.bfloat16),
        "frame",
        scatter_dimension=0,
        tiled=True,
    ).astype(jnp.float32)
    return (summed + mixed_tokens.astype(jnp.float32)).astype(jnp.bfloat16)


def solution(mesh):
    placed = (
        P(None, "row", "frame", None),
        P("frame", "row", None, None),
        P(),
        P(),
        P(),
        P(None, None, "frame"),
        P("frame", None),
    )
    return jax.shard_map(
        local, mesh=mesh, in_specs=placed, out_specs=P("frame", "row", None, None), check_vma=False
    )
```

profile of v0, /device:TPU:1, one launch (start us, length us, event | category | flops | bytes accessed | tf_op | source)
XLA Modules:
  0.0 413.1 jit_solution(9065503412043573236)
XLA Ops:
  8.4 18.0 %all_to_all.4 = bf16[8,8,2,3072]{3,2,1,0:T(2,128)(2,1)S(1)} all-to-all(bf16[8,8,2,3072]{3,2,1,0:T(2,128)(2,1)S(1)} %reshape.73), channel_id=1, replica_groups=mesh['frame'=8,'row'=16] {'frame'}, dimensions={0} | all-to-all | bytes 1572864 | tf_op jit(solution)/shard_map/all_to_all | solution.py:76
  28.3 3.2 reshape.79
  34.3 3.8 collective-permute-start.1
  38.1 3.1 collective-permute-start
  41.2 7.7 %collective-permute-done.1 = bf16[1,8,16,3072]{3,2,1,0:T(8,128)(2,1)S(1)} collective-permute-done((bf16[1,8,16,3072]{3,2,1,0:T(8,128)(2,1)S(1)}, bf16[1,8,16,3072]{3,2,1,0:T(8,128)(2,1)S(1)}, u32[]{:S(2)}, u32[]{:S(2)}) %collective-permute-start.1) | collective-permute-done | bytes 786464 | tf_op jit(solution)/shard_map/ppermute | solution.py:19
  53.1 191.4 %all-gather.2.cloned.1.call-done = bf16[8,24,16,3072]{3,2,1,0:T(8,128)(2,1)} async-done(((bf16[1,24,16,3072]{3,2,1,0:T(8,128)(2,1)}), bf16[8,24,16,3072]{3,2,1,0:T(8,128)(2,1)}) %all-gather.2.cloned.1.call-update) | async-done | bytes 18874384 | tf_op jit(solution)/shard_map/all_gather | solution.py:87
  244.5 6.9 %fusion.34 = bf16[8,8,16,384]{3,2,1,0:T(8,128)(2,1)S(1)} fusion(bf16[8,24,16,3072]{3,2,1,0:T(8,128)(2,1)} %all-gather.2.cloned.1.call-done, bf16[3072,3,384]{2,0,1:T(8,128)(2,1)} %param.16), kind=kOutput, calls=%fused_computation.45 | convolution fusion | flops 2416312320 | bytes 22020096 | tf_op jit(solution)/shard_map/frcd,dh->frch/dot_general | solution.py:90
  253.1 19.3 %fusion.21 = bf16[8,24,16,2,384]{4,2,3,1,0:T(8,128)(2,1)S(1)} fusion(bf16[3072,3,384]{2,0,1:T(8,128)(2,1)} %param.16, bf16[8,24,16,3072]{3,2,1,0:T(8,128)(2,1)} %all-gather.2.cloned.1.call-done), kind=kOutput, calls=%fused_computation.26 | convolution fusion | flops 14497873920 | bytes 28311552 | tf_op jit(solution)/shard_map/frcd,dkh->frckh/dot_general | solution.py:93
  272.4 5.7 %fusion.18 = bf16[8,24,16,2,384]{4,2,3,1,0:T(8,128)(2,1)} fusion(s32[]{:T(128)S(6)} %select_n.38, bf16[8,24,16,2,384]{4,2,3,1,0:T(8,128)(2,1)S(1)} %fusion.21), kind=kLoop, calls=%fused_computation.23 | loop fusion | flops 9437184 | bytes 9437188 | tf_op jit(solution)/shard_map/jit(_roll_dynamic)/concatenate | solution.py:36
  278.2 12.9 %reshape.76 = bf16[8,24,2,8,2,3,128]{6,5,3,2,4,1,0:T(4,128)(2,1)} reshape(bf16[8,24,16,2,384]{4,2,3,1,0:T(8,128)(2,1)} %fusion.18) | data formatting | bytes 9437184 | tf_op jit(solution)/shard_map/reshape | solution.py:41
  291.1 5.1 %fusion.44 = (bf16[1,2,3,8,24,8,128]{6,2,5,1,0,4,3:T(4,128)(2,1)S(1)}, bf16[1,2,3,8,24,8,128]{6,2,5,1,0,4,3:T(4,128)(2,1)S(1)}) fusion(bf16[2,2,3,8,24,8,128]{6,2,5,1,0,4,3:T(4,128)(2,1)} %bitcast.83), kind=kLoop, calls=%fused_computation.57 | loop fusion | bytes 9437184 | tf_op jit(solution)/shard_map/slice | solution.py:66
  296.2 2.0 copy.19
  298.3 2.0 copy.20
  300.3 26.3 %while.11 = (s32[]{:T(128)}, bf16[6,512,128]{2,1,0:T(8,128)(2,1)S(1)}, bf16[6,512,128]{2,1,0:T(8,128)(2,1)}, bf16[6,1536,128]{2,1,0:T(8,128)(2,1)}, bf16[6,1536,...) while((s32[]{:T(128)}, ...), condition=%wide.region_4.6_spmd.clone, body=%wide.region_1.5_spmd.clone.sunk | while | flops 410582016 | bytes 10507877 | solution.py:66
  300.3 2.0 fusion.51
  302.9 1.8 fusion.53
  304.7 2.0 fusion.51
  309.1 2.0 fusion.51
  313.4 2.0 fusion.51
  317.8 2.0 fusion.51
  322.2 2.0 fusion.51
  326.7 5.4 %convolution_convert_fusion = bf16[8,8,16,3072]{3,2,1,0:T(8,128)(2,1)} fusion(bf16[384,3072]{1,0:T(8,128)(2,1)S(1)} %copy-done, s32[]{:T(128)S(6)} %select_n.40, bf16[8,8,16,384]{3,2,1,0:T(8,128)(2,1)S(1)} %bitcast.88), kind=kOutput, calls=%fused_computation.22 | convolution fusion | flops 2420637696 | bytes 9437188 | tf_op jit(solution)/shard_map/frck,ke->frce/dot_general | solution.py:115
  332.2 71.9 %reduce-scatter.2.cloned.1.call-done = bf16[1,8,16,3072]{3,2,1,0:T(8,128)(2,1)} async-done(((bf16[8,8,16,3072]{3,2,1,0:T(8,128)(2,1)}), bf16[1,8,16,3072]{3,2,1,0:T(8,128)(2,1)}) %reduce-scatter.2.cloned.1.call-update) | async-done | bytes 786448 | tf_op jit(solution)/shard_map/reduce_scatter | solution.py:114
  404.1 2.2 fusion.33
  (48 shorter events, 24.1 us)
Async XLA Ops:
  6.5 320.2 %copy-start = (bf16[384,3072]{1,0:T(8,128)(2,1)S(1)}, bf16[384,3072]{1,0:T(8,128)(2,1)}, u32[]{:S(2)}) copy-start(bf16[384,3072]{1,0:T(8,128)(2,1)} %param.17) | copy-start | bytes 7077892
  6.5 238.0 %all-gather.2.cloned.1.call-start = ((), (), s32[]{:S(2)}) async-start(), calls=%async_computation.2 | async-start | bytes 21233664 | tf_op jit(solution)/shard_map/all_gather | solution.py:87
  26.9 4.5 %copy-start.3 = (bf16[1,8,16,3072]{3,2,1,0:T(8,128)(2,1)S(1)}, bf16[1,8,16,3072]{3,2,1,0:T(8,128)(2,1)}, u32[]{:S(2)}) copy-start(bf16[1,8,16,3072]{3,2,1,0:T(8,128)(2,1)} %param.12) | copy-start | bytes 2359300
  28.3 5.8 %copy-start.4 = (f32[3072]{0:T(1024)S(1)}, f32[3072]{0:T(1024)}, u32[]{:S(2)}) copy-start(f32[3072]{0:T(1024)} %param.15) | copy-start | bytes 36868
  33.1 0.9 copy-start.1
  34.3 18.2 %copy-start.5 = (s32[128]{0:T(128)S(1)}, s32[128]{0:T(128)}, u32[]{:S(2)}) copy-start(s32[128]{0:T(128)} %param.13) | copy-start | bytes 1540
  34.3 14.6 %collective-permute-start.1 = (bf16[1,8,16,3072]{3,2,1,0:T(8,128)(2,1)S(1)}, bf16[1,8,16,3072]{3,2,1,0:T(8,128)(2,1)S(1)}, u32[]{:S(2)}, u32[]{:S(2)}) collective-permute-start(bf16[1,8,16,3072]{3,2,1,0:T(8,128)(2,1)S(1)} %fusion.32), channel_id=1, source_target_pairs={{1,0},{2,1},{3,2},{4,3},{5,4},{6,5},{7,6},{8,7},{9,8},{10,9},{11,1... | collective-permute-start | bytes 2359304 | tf_op jit(solution)/shard_map/ppermute | solution.py:19
  38.1 12.0 %collective-permute-start = (bf16[1,8,16,3072]{3,2,1,0:T(8,128)(2,1)S(1)}, bf16[1,8,16,3072]{3,2,1,0:T(8,128)(2,1)S(1)}, u32[]{:S(2)}, u32[]{:S(2)}) collective-permute-start(bf16[1,8,16,3072]{3,2,1,0:T(8,128)(2,1)S(1)} %fusion.32), channel_id=1, source_target_pairs={{0,1},{1,2},{2,3},{3,4},{4,5},{5,6},{6,7},{7,8},{8,9},{9,10},{10,1... | collective-permute-start | bytes 2359304 | tf_op jit(solution)/shard_map/ppermute | solution.py:16
  51.8 352.3 %reduce-scatter.2.cloned.1.call-start = ((), (), s32[]{:S(2)}) async-start(), calls=%async_computation.3 | async-start | bytes 7077888 | tf_op jit(solution)/shard_map/reduce_scatter | solution.py:114
  332.2 71.9 %copy-start.2 = (bf16[1,8,16,3072]{3,2,1,0:T(8,128)(2,1)S(1)}, bf16[1,8,16,3072]{3,2,1,0:T(8,128)(2,1)}, u32[]{:S(2)}) copy-start(bf16[1,8,16,3072]{3,2,1,0:T(8,128)(2,1)} %copy-done.1) | copy-start | bytes 2359300
Sparse Core Ops, SparseCore 0:
  51.9 192.5 all-gather.1
  332.3 71.7 reduce-scatter.1
where the time goes:
time: 414 us; the launch traced here: 413 us
  waiting for transfers between devices  272 us (66%)
  matrix products  54.3 us (13%)
  local copies, waits for them, and re-layouts  31.1 us (8%)
  blocking collectives  18 us (4%)
  other arithmetic  16.1 us (4%)
  between operations  14.3 us (3%)
  starting transfers between devices  6.92 us (2%)
    all_gather x1, waiting for transfers between devices, local(): piece = lax.all_gather(rim_tokens, 'frame', axis=0, tiled=True)  191 us
    reduce_scatter x1, waiting for transfers between devices, local(): lax.psum_scatter(jnp.einsum('frck,ke->frce', attended, project_out, prefe...  71.9 us
    dot_general x1, matrix products, local(): jnp.einsum('frcd,dkh->frckh', piece, pair_weight, preferred_element_type=...  19.3 us
    all_to_all x1, blocking collectives, local(): lax.all_to_all(fine_tokens, 'frame', split_axis=0, concat_axis=2, tiled=T...  18 us
    reshape x1, local copies, waits for them, and re-layouts, window_attention(): keyval.reshape(frame_count, key_rows, windows, WIN_COLS, 2, head_count, H...  12.9 us
    dot_general x6, matrix products, one_block(): jnp.dot(query_block, key_block.T, preferred_element_type=jnp.float32)  12.1 us
    dot_general x6, matrix products, one_block(): jnp.dot(weights, value_block, preferred_element_type=jnp.float32)  10.6 us
    slice x3, local copies, waits for them, and re-layouts, window_attention(): results = lax.map(one_block, (query_blocks, pair_blocks[0], pair_blocks[1]))  9.2 us
  transfers between devices with their start and end apart: 4, of which 4 were waited for; matrix products, arithmetic and copies ran while one was open for 0% of the time, Pallas kernels for 0%

commit v1 on v0

v1 whole, which is shorter than its diff:
```python
import functools

import jax
import jax.numpy as jnp
from jax import lax
from jax.experimental import pallas as pl
from jax.experimental.pallas import tpu as pltpu
from jax.sharding import PartitionSpec as P

MESH = pl.DeviceIdType.MESH
HEAD = 128
D = 3072
TOK = 128
QTR = 32
WIDTH = 384
CHUNK = 768
N_FIRST = 2
BF = jnp.bfloat16
F32 = jnp.float32


def place():
    frame = lax.axis_index("frame")
    row = lax.axis_index("row")
    return frame // 4, frame % 4, row


def packed_columns(shift, shape, dim):
    token = lax.broadcasted_iota(jnp.int32, shape, dim)
    position = (token // 64) * 8 + token % 8
    column = position + shift
    column = jnp.where(column >= 16, column - 16, column)
    return (token // 8) % 8, column


def gather_kernel(
    base_ref, deg_ref, shift_ref, gain_ref, win_ref, wout_ref,
    mixed_ref, q_ref, kv_ref, wpair_ref,
    g, b, w, base_sem, x_send, z_send, g_recv, kv_send, kv_recv, w_sem, wo_sem,
):
    z, x, row = place()
    me = z * 4 + x
    other = (1 - z) * 4
    right, left, opp = lax.rem(x + 1, 4), lax.rem(x + 3, 4), lax.rem(x + 2, 4)
    mate = row + 1 - 2 * lax.rem(row, 2)
    far_row = lax.rem(row + 8, 16)

    copies = []
    for k in range(3):
        copy = pltpu.make_async_copy(win_ref.at[k], w.at[k], w_sem.at[k])
        copy.start()
        copies.append(copy)

    barrier = pltpu.get_barrier_semaphore()
    for step in range(1, 8):
        pl.semaphore_signal(
            barrier, inc=1, device_id=(lax.rem(me + step, 8), row), device_id_type=MESH
        )
    for target in ((me, mate), (other + x, far_row)):
        pl.semaphore_signal(barrier, inc=1, device_id=target, device_id_type=MESH)
    outer = row + 2 * lax.rem(row, 2) - 1
    has_outer = jnp.logical_and(outer >= 0, outer < 16)

    @pl.when(has_outer)
    def _():
        pl.semaphore_signal(barrier, inc=1, device_id=(me, outer), device_id_type=MESH)
        pl.semaphore_wait(barrier, 10)

    @pl.when(jnp.logical_not(has_outer))
    def _():
        pl.semaphore_wait(barrier, 9)

    sends = []

    def remote(src, dst, send, recv, target):
        copy = pltpu.make_async_remote_copy(
            src_ref=src, dst_ref=dst, send_sem=send, recv_sem=recv,
            device_id=target, device_id_type=MESH,
        )
        copy.start()
        return copy

    base_copies = []
    for step in range(1, 8):
        to = lax.rem(me + step, 8)
        base_copies.append(
            remote(base_ref.at[to], b.at[me], base_sem.at[0, step], base_sem.at[1, step], (to, row))
        )
    own_base = pltpu.make_async_copy(base_ref.at[me], b.at[me], base_sem.at[0, 0])
    own_base.start()

    half = WIDTH // 2
    core = lax.rem(row, 2)
    mine = pl.ds(pl.multiple_of(core * half, half), half)
    w_first = remote(
        wout_ref.at[mine], wpair_ref.at[mine], wo_sem.at[0], wo_sem.at[1], (other + x, far_row)
    )

    shift = shift_ref[0]
    rows_q, cols_q = packed_columns(shift, (TOK, TOK), 0)
    source = lax.broadcasted_iota(jnp.int32, (TOK, TOK), 1)
    pick_fine = (source == rows_q * 16 + cols_q).astype(F32).astype(BF)

    own_base.wait()
    for copy in base_copies:
        copy.wait()

    square = jnp.zeros((TOK, 1), F32)
    for c in range(4):
        lanes = slice(c * CHUNK, (c + 1) * CHUNK)
        pick_base = (source == (cols_q // 2) * 16 + c * 4 + rows_q // 2).astype(F32).astype(BF)
        total = jnp.dot(pick_fine, deg_ref[:, lanes], preferred_element_type=F32) + jnp.dot(
            pick_base, b[...].reshape(TOK, CHUNK), preferred_element_type=F32
        )
        total = total.astype(BF)
        mixed_ref[:, lanes] = total
        total = total.astype(F32)
        square = square + jnp.sum(total * total, axis=1, keepdims=True)
    scale = lax.rsqrt(square * (1.0 / D) + 1e-06)
    for c in range(4):
        lanes = slice(c * CHUNK, (c + 1) * CHUNK)
        normed = mixed_ref[:, lanes].astype(F32) * scale * gain_ref[:, lanes]
        g[me, :, :, lanes] = normed.astype(BF).reshape(4, QTR, CHUNK)

    def item(plane, column):
        return (z * 4 if plane == 0 else other) + column

    def x_push(direction, plane, column, t, forward):
        frame = item(plane, column)
        to = right if direction == 0 else left
        sends.append(
            remote(g.at[frame, t], g.at[frame, t], x_send.at[direction, plane, forward, t],
                   g_recv.at[frame, t], (z * 4 + to, row))
        )

    def z_push(slot, column, t):
        frame = item(0, column)
        sends.append(
            remote(g.at[frame, t], g.at[frame, t], z_send.at[slot, t],
                   g_recv.at[frame, t], (other + x, row))
        )

    def arrive(plane, column, t):
        frame = item(plane, column)
        pltpu.make_async_remote_copy(
            src_ref=g.at[frame, t], dst_ref=g.at[frame, t], send_sem=z_send.at[0, 0],
            recv_sem=g_recv.at[frame, t], device_id=(other + x, row), device_id_type=MESH,
        ).wait_recv()

    kv_up, kv_down = [], []

    def project(plane, column):
        frame = item(plane, column)
        tokens = g[frame].reshape(TOK, D)
        q_ref[frame] = jnp.dot(tokens, w[0], preferred_element_type=F32).astype(BF)
        kv_ref[1, frame, :, :WIDTH] = jnp.dot(tokens, w[1], preferred_element_type=F32).astype(BF)
        kv_ref[1, frame, :, WIDTH:] = jnp.dot(tokens, w[2], preferred_element_type=F32).astype(BF)
        n = len(kv_up)
        up = pltpu.make_async_remote_copy(
            src_ref=kv_ref.at[1, frame], dst_ref=kv_ref.at[0, frame], send_sem=kv_send.at[0, n],
            recv_sem=kv_recv.at[0, n], device_id=(me, row + 1), device_id_type=MESH,
        )
        down = pltpu.make_async_remote_copy(
            src_ref=kv_ref.at[1, frame], dst_ref=kv_ref.at[2, frame], send_sem=kv_send.at[1, n],
            recv_sem=kv_recv.at[1, n], device_id=(me, row - 1), device_id_type=MESH,
        )
        kv_up.append(up)
        kv_down.append(down)

        @pl.when(row < 15)
        def _():
            up.start()

        @pl.when(row > 0)
        def _():
            down.start()

    first = range(N_FIRST)
    late = range(N_FIRST, 4)
    for t in range(4):
        if t in first:
            z_push(0, x, t)
        x_push(0, 0, x, t, 0)
        x_push(1, 0, x, t, 0)
    for t in late:
        z_push(0, x, t)

    @pl.when(row == 0)
    def _():
        kv_ref[0] = jnp.zeros(kv_ref.shape[1:], BF)

    @pl.when(row == 15)
    def _():
        kv_ref[2] = jnp.zeros(kv_ref.shape[1:], BF)

    for copy in copies:
        copy.wait()
    project(0, x)
    for t in range(4):
        if t in first:
            arrive(1, x, t)
            x_push(0, 1, x, t, 0)
            x_push(1, 1, x, t, 0)
        arrive(0, left, t)
        if t % 2 == 0:
            x_push(0, 0, left, t, 1)
        if t in late:
            z_push(1, left, t)
        arrive(0, right, t)
        if t % 2 == 1:
            x_push(1, 0, right, t, 1)
        if t in late:
            z_push(2, right, t)
    project(0, left)
    for t in first:
        arrive(1, left, t)
        if t % 2 == 1:
            x_push(0, 1, left, t, 1)
        arrive(1, right, t)
        if t % 2 == 0:
            x_push(1, 1, right, t, 1)
    for t in late:
        arrive(0, opp, t)
        z_push(3, opp, t)
    project(0, right)
    for t in first:
        arrive(0, opp, t)
    project(0, opp)
    w_first.wait_recv()
    w_second = remote(
        wpair_ref.at[mine], wpair_ref.at[mine], wo_sem.at[2], wo_sem.at[3], (me, mate)
    )
    for t in late:
        arrive(1, x, t)
    project(1, x)
    for t in late:
        arrive(1, left, t)
    project(1, left)
    for t in late:
        arrive(1, right, t)
    project(1, right)
    for t in range(4):
        arrive(1, opp, t)
    project(1, opp)

    for copy in sends:
        copy.wait_send()
    w_first.wait_send()
    w_second.wait()

    @pl.when(row < 15)
    def _():
        for copy in kv_up:
            copy.wait_send()
        for copy in kv_down:
            copy.wait_recv()

    @pl.when(row > 0)
    def _():
        for copy in kv_down:
            copy.wait_send()
        for copy in kv_up:
            copy.wait_recv()


def attention_kernel(rw_ref, q_ref, kv_ref, out_ref, bias):
    keys = 3 * 8 * 64
    first = lax.axis_index("row") * 8
    place_of = lax.broadcasted_iota(jnp.int32, (1, keys), 1)
    key_row = (place_of // 512) * 8 + (place_of % 64) // 8
    key_ids = jnp.full((1, keys), -1, jnp.int32)
    for r in range(24):
        row = first + r - 8
        inside = jnp.logical_and(row >= 0, row < 128)
        number = jnp.where(inside, rw_ref[jnp.clip(row, 0, 127)], -1)
        key_ids = jnp.where(key_row == r, number, key_ids)
    for r in range(8):
        line = jnp.where(key_ids == rw_ref[first + r], 0.0, -1e30)
        line = jnp.broadcast_to(line, (8, keys))
        bias[pl.ds(8 * r, 8), :] = line
        bias[pl.ds(64 + 8 * r, 8), :] = line
    factor = HEAD ** (-0.5) * 1.4426950408889634
    for c in range(2):
        for h in range(3):
            key = kv_ref[:, :, c * 64 : c * 64 + 64, h * HEAD : (h + 1) * HEAD].reshape(keys, HEAD)
            value = kv_ref[
                :, :, c * 64 : c * 64 + 64, WIDTH + h * HEAD : WIDTH + (h + 1) * HEAD
            ].reshape(keys, HEAD)

            def block(i, carry):
                at = pl.ds(i * 2, 2)
                query = q_ref[at, c * 64 : c * 64 + 64, h * HEAD : (h + 1) * HEAD].reshape(
                    128, HEAD
                )
                scores = lax.dot_general(
                    query, key, (((1,), (1,)), ((), ())), preferred_element_type=F32
                )
                scores = scores + bias[...]
                highest = jnp.max(scores, axis=1, keepdims=True)
                raised = jnp.exp2((scores - highest) * factor)
                total = jnp.sum(raised, axis=1, keepdims=True)
                result = jnp.dot(raised.astype(BF), value, preferred_element_type=F32)
                result = (result * (1.0 / total)).astype(BF)
                out_ref[at, c * 64 : c * 64 + 64, h * HEAD : (h + 1) * HEAD] = result.reshape(
                    2, 64, HEAD
                )
                return carry

            lax.fori_loop(0, 4, block, 0)


def scatter_kernel(
    shift_ref, att_ref, mixed_ref, wown_ref, wpair_ref, out_ref,
    pair, w, part, inbox, z_sem, send, recv, w_sem,
):
    z, x, row = place()
    me = z * 4 + x
    other = (1 - z) * 4
    right, left, opp = lax.rem(x + 1, 4), lax.rem(x + 3, 4), lax.rem(x + 2, 4)
    loads = []
    for k, source in enumerate((wown_ref, wpair_ref)):
        copy = pltpu.make_async_copy(source, w.at[pl.ds(k * WIDTH, WIDTH)], w_sem.at[k])
        copy.start()
        loads.append(copy)

    barrier = pltpu.get_barrier_semaphore()
    for target in (other + x, z * 4 + right, z * 4 + left):
        pl.semaphore_signal(barrier, inc=1, device_id=(target, row), device_id_type=MESH)
    pl.semaphore_wait(barrier, 3)

    def remote(src, dst, s, r, target):
        copy = pltpu.make_async_remote_copy(
            src_ref=src, dst_ref=dst, send_sem=s, recv_sem=r,
            device_id=(target, row), device_id_type=MESH,
        )
        copy.start()
        return copy

    order = (opp, right, left, x)
    crossing = [
        remote(att_ref.at[other + c], pair.at[k], z_sem.at[0, k], z_sem.at[1, k], other + x)
        for k, c in enumerate(order)
    ]
    for copy in loads:
        copy.wait()

    def compute(k):
        crossing[k].wait_recv()
        tokens = jnp.concatenate([att_ref[z * 4 + order[k]], pair[k]], axis=1)
        for c in range(4):
            lanes = slice(c * CHUNK, (c + 1) * CHUNK)
            part[k, :, :, lanes] = (
                jnp.dot(tokens, w[:, lanes], preferred_element_type=F32)
                .astype(BF)
                .reshape(2, 64, CHUNK)
            )

    def push(direction, slot, k, h):
        to = z * 4 + (right if direction == 0 else left)
        return remote(
            part.at[k, h], inbox.at[direction, slot], send.at[direction, slot],
            recv.at[direction, slot], to,
        )

    compute(0)
    rights = [push(0, 0, 0, 0)]
    lefts = [push(1, 0, 0, 1)]
    compute(1)
    rights.append(push(0, 1, 1, 1))
    compute(2)
    lefts.append(push(1, 1, 2, 0))
    rights[0].wait_recv()
    part[1, 0] = (part[1, 0].astype(F32) + inbox[0, 0].astype(F32)).astype(BF)
    rights.append(push(0, 2, 1, 0))
    lefts[0].wait_recv()
    part[2, 1] = (part[2, 1].astype(F32) + inbox[1, 0].astype(F32)).astype(BF)
    lefts.append(push(1, 2, 2, 1))
    compute(3)

    shift = shift_ref[0]
    rows_p, cols_p = packed_columns(shift, (TOK, TOK), 1)
    target_token = lax.broadcasted_iota(jnp.int32, (TOK, TOK), 0)
    unpick = (target_token == rows_p * 16 + cols_p).astype(F32).astype(BF)
    rights[1].wait_recv()
    lefts[1].wait_recv()
    rights[2].wait_recv()
    lefts[2].wait_recv()
    for c in range(4):
        lanes = slice(c * CHUNK, (c + 1) * CHUNK)
        a, bb = (
            part[3, 0, :, lanes].astype(F32)
            + inbox[0, 2, :, lanes].astype(F32)
            + inbox[1, 1, :, lanes].astype(F32),
            part[3, 1, :, lanes].astype(F32)
            + inbox[0, 1, :, lanes].astype(F32)
            + inbox[1, 2, :, lanes].astype(F32),
        )
        total = jnp.concatenate([a, bb], axis=0) + mixed_ref[:, lanes].astype(F32)
        out_ref[:, lanes] = jnp.dot(
            unpick, total.astype(BF), preferred_element_type=F32
        ).astype(BF)
    for copy in crossing + rights + lefts:
        copy.wait_send()


VM = pl.BlockSpec(memory_space=pltpu.VMEM)
SM = pl.BlockSpec(memory_space=pltpu.SMEM)
ANY = pl.BlockSpec(memory_space=pl.ANY)
DMA = pltpu.SemaphoreType.DMA


def local(base_latent, degraded, row_window, column_shift, norm_gain, project_in, project_out):
    base = base_latent.reshape(8, 4, 4, CHUNK).transpose(0, 2, 1, 3).reshape(8, 16, CHUNK)
    fine = degraded.reshape(TOK, D)
    weights = project_in.transpose(1, 0, 2)
    mixed, query, keyval, wpair = pl.pallas_call(
        gather_kernel,
        out_shape=(
            jax.ShapeDtypeStruct((TOK, D), BF),
            jax.ShapeDtypeStruct((8, TOK, WIDTH), BF),
            jax.ShapeDtypeStruct((3, 8, TOK, 2 * WIDTH), BF),
            jax.ShapeDtypeStruct((WIDTH, D), BF),
        ),
        in_specs=[VM, VM, SM, VM, ANY, ANY],
        out_specs=(VM, VM, VM, ANY),
        scratch_shapes=[
            pltpu.VMEM((8, 4, QTR, D), BF),
            pltpu.VMEM((8, 16, CHUNK), BF),
            pltpu.VMEM((3, D, WIDTH), BF),
            DMA((2, 8)),
            DMA((2, 2, 2, 4)),
            DMA((4, 4)),
            DMA((8, 4)),
            DMA((2, 8)),
            DMA((2, 8)),
            DMA((3,)),
            DMA((4,)),
        ],
        compiler_params=pltpu.CompilerParams(
            collective_id=0, has_side_effects=True, vmem_limit_bytes=56 * 2**20
        ),
        name="gather_project",
    )(base, fine, column_shift, norm_gain.reshape(1, D), weights, project_out)
    attended = pl.pallas_call(
        attention_kernel,
        out_shape=jax.ShapeDtypeStruct((8, TOK, WIDTH), BF),
        in_specs=[SM, VM, VM],
        out_specs=VM,
        scratch_shapes=[pltpu.VMEM((128, 1536), F32)],
        compiler_params=pltpu.CompilerParams(vmem_limit_bytes=48 * 2**20),
        name="attend",
    )(row_window, query, keyval)
    out = pl.pallas_call(
        scatter_kernel,
        out_shape=jax.ShapeDtypeStruct((TOK, D), BF),
        in_specs=[SM, VM, VM, ANY, ANY],
        out_specs=VM,
        scratch_shapes=[
            pltpu.VMEM((4, TOK, WIDTH), BF),
            pltpu.VMEM((2 * WIDTH, D), BF),
            pltpu.VMEM((4, 2, 64, D), BF),
            pltpu.VMEM((2, 3, 64, D), BF),
            DMA((2, 4)),
            DMA((2, 3)),
            DMA((2, 3)),
            DMA((2,)),
        ],
        compiler_params=pltpu.CompilerParams(
            collective_id=1, has_side_effects=True, vmem_limit_bytes=56 * 2**20
        ),
        name="project_scatter",
    )(column_shift, attended, mixed, project_out, wpair)
    return out.reshape(1, 8, 16, D)


def solution(mesh):
    placed = (
        P(None, "row", "frame", None),
        P("frame", "row", None, None),
        P(),
        P(),
        P(),
        P(None, None, "frame"),
        P("frame", None),
    )
    return jax.shard_map(
        local, mesh=mesh, in_specs=placed, out_specs=P("frame", "row", None, None), check_vma=False
    )
```

time: 414 us -> 140 us (0.34)
  waiting for transfers between devices: 272 us -> 0 us
  Pallas kernels: 0 us -> 132 us
  matrix products: 54.3 us -> 0 us
  local copies, waits for them, and re-layouts: 31.1 us -> 5.72 us
  blocking collectives: 18 us -> 0 us
  other arithmetic: 16.1 us -> 0 us
  between operations: 14.3 us -> 0.7 us
  starting transfers between devices: 6.92 us -> 0 us
    all_gather x1 -> x0, waiting for transfers between devices: 191 us -> none  [local(): piece = lax.all_gather(rim_tokens, 'frame', axis=0, tiled=True)]
    pallas_call x0 -> x3, Pallas kernels: none -> 132 us  [the longest x1 78.8 us: local(): pl.pallas_call(gather_kernel, out_shape=(jax.ShapeDtypeStruct((TOK, D), B...]
    reduce_scatter x1 -> x0, waiting for transfers between devices: 71.9 us -> none  [local(): lax.psum_scatter(jnp.einsum('frck,ke->frce', attended, project_out, prefe...]
    dot_general x15 -> x0, matrix products: 54.3 us -> none  [the longest x1 19.3 us: local(): jnp.einsum('frcd,dkh->frckh', piece, pair_weight, preferred_element_type=...]
    all_to_all x1 -> x0, blocking collectives: 18 us -> none  [local(): lax.all_to_all(fine_tokens, 'frame', split_axis=0, concat_axis=2, tiled=T...]
    reshape x3 -> x1, local copies, waits for them, and re-layouts: 13.5 us -> 1.65 us  [local(): base_latent.reshape(8, 4, 4, CHUNK).transpose(0, 2, 1, 3)]
    slice x3 -> x0, local copies, waits for them, and re-layouts: 9.2 us -> none  [window_attention(): results = lax.map(one_block, (query_blocks, pair_blocks[0], pair_blocks[1]))]
    ppermute x2 -> x0, waiting for transfers between devices: 8.91 us -> none  [the longest x1 7.73 us: extended(): lax.ppermute(lax.slice_in_dim(block, 0, width, axis=dim), axis, backward)]
  transfers between devices with their start and end apart: 4 -> 0, of which waited for: 4 -> 0; matrix products, arithmetic and copies ran while one was open for 0% -> 0% of each run, Pallas kernels for 0% -> 0%
where the time goes in v1:
time: 140 us; the launch traced here: 139 us
  Pallas kernels  132 us (94%)
  local copies, waits for them, and re-layouts  5.72 us (4%)
    pallas_call x1, Pallas kernels, local(): pl.pallas_call(gather_kernel, out_shape=(jax.ShapeDtypeStruct((TOK, D), B...  78.8 us
    pallas_call x1, Pallas kernels, local(): pl.pallas_call(scatter_kernel, out_shape=jax.ShapeDtypeStruct((TOK, D), B...  35.2 us
    pallas_call x1, Pallas kernels, local(): pl.pallas_call(attention_kernel, out_shape=jax.ShapeDtypeStruct((8, TOK,...  18.4 us
    unnamed x7, local copies, waits for them, and re-layouts  4.07 us

profile of v1, /device:TPU:1, one launch (start us, length us, event | category | flops | bytes accessed | tf_op | source)
XLA Modules:
  0.0 138.8 jit_solution(11352745219998951092)
XLA Ops:
  0.7 1.7 %reshape.16.base_ref = bf16[8,16,768]{2,1,0:T(8,128)(2,1)} reshape(bf16[8,4,4,768]{3,2,1,0:T(4,128)(2,1)} %bitcast.10) | data formatting | bytes 393216 | tf_op jit(solution)/shard_map/reshape | solution.py:413
  2.3 0.0 copy-start.2
  2.3 78.8 %gather_project.1 = (bf16[128,3072]{1,0:T(8,128)(2,1)}, bf16[8,128,384]{2,1,0:T(8,128)(2,1)}, bf16[3,8,128,768]{3,2,1,0:T(8,128)(2,1)}, bf16[384,3072]{1,0:T(8,128)(2,1)}) custom-call(bf16[8,16,768]{2,1,0:T(8,128)(2,1)} %reshape.16.base_ref, bf16[128,3072]{1,0:T(8,128)(2,1)} %bitcast.9, s32[1]{0:T(128)S(6)} %copy.10.shift_ref, f32[1,3072]{1,0:T(1,128)} %bitcast.11, ...), custom_call_target="tpu_custom_call" | custom-call | tf_op jit(solution)/shard_map/gather_project/pallas_call | solution.py:416
  81.1 0.0 copy-done.2
  81.1 0.0 copy-start.1
  81.1 1.1 copy-done.1
  82.2 18.4 %attend.1.att_ref = bf16[8,128,384]{2,1,0:T(8,128)(2,1)S(1)} custom-call(s32[128]{0:T(128)S(1)} %copy-done.2, bf16[8,128,384]{2,1,0:T(8,128)(2,1)S(1)} %copy-done.1, bf16[3,8,128,768]{3,2,1,0:T(8,128)(2,1)} %get-tuple-element.10.kv_ref), custom_call_target="tpu_custom_call" | custom-call | tf_op jit(solution)/shard_map/attend/pallas_call | solution.py:444
  100.6 0.0 copy-start
  100.7 0.9 copy-done
  101.5 35.2 %project_scatter.1 = bf16[128,3072]{1,0:T(8,128)(2,1)} custom-call(s32[1]{0:T(128)S(6)} %copy.10.shift_ref, bf16[8,128,384]{2,1,0:T(8,128)(2,1)} %copy-done, bf16[128,3072]{1,0:T(8,128)(2,1)} %get-tuple-element.11.mixed_ref, bf16[384,3072]{1,0:T(8,128)(2,1)} %wown_ref.1, bf16[384,3072]{1,0:T(8,128)(2,1)} %get-tuple-element.12.wpair_ref), custom_call_target="tpu_custom_call" | custom-call | tf_op jit(solution)/shard_map/project_scatter/pallas_call | solution.py:453
  136.8 2.1 %copy.11 = bf16[1,8,16,3072]{3,2,1,0:T(8,128)(2,1)} copy(bf16[1,8,16,3072]{3,2,1,0:T(8,128)(2,1)} %bitcast.8) | data formatting | bytes 1572864
Async XLA Ops:
  2.3 78.8 %copy-start.2 = (s32[128]{0:T(128)S(1)}, s32[128]{0:T(128)}, u32[]{:S(2)}) copy-start(s32[128]{0:T(128)} %rw_ref.1) | copy-start | bytes 1540
  81.1 1.1 copy-start.1
  100.6 0.9 copy-start

commit v2 on v0

v2 whole, which is shorter than its diff:
```python
import jax
import jax.numpy as jnp
from jax import lax
from jax.experimental import pallas as pl
from jax.experimental.pallas import tpu as pltpu
from jax.sharding import PartitionSpec as P

MESH = pl.DeviceIdType.MESH
HEAD = 128
D = 3072
TOK = 128
SIDE = 64
QTR = 32
WIDTH = 384
CHUNK = 768
BF = jnp.bfloat16
F32 = jnp.float32
FACTOR = HEAD ** (-0.5) * 1.4426950408889634


def packed_place(shift, token):
    column = (token // SIDE) * 8 + token % 8 + shift
    column = jnp.where(column >= 16, column - 16, column)
    return (token // 8) % 8, column


def one_hot(mask):
    return jnp.where(mask, 1.0, 0.0).astype(BF)


def layer_kernel(
    base_ref, deg_ref, shift_ref, rw_ref, gain_ref, win_ref, wout_ref,
    out_ref,
    g, b, w, wo, mixed, q, kv, att, pair, part, inbox, bias_own, bias_rim,
    base_sem, x_send, z_send, g_recv, kv_send, kv_recv, w_sem, wo_sem,
    pair_send, pair_recv, part_send, part_recv,
):
    row = lax.axis_index("row")
    me = lax.axis_index("frame")
    z, x = me // 4, me % 4
    here, other = z * 4, (1 - z) * 4
    right, left, opp = lax.rem(x + 1, 4), lax.rem(x + 3, 4), lax.rem(x + 2, 4)
    mate = row + 1 - 2 * lax.rem(row, 2)
    outer = row + 2 * lax.rem(row, 2) - 1
    far_row = lax.rem(row + 8, 16)

    loads = []
    for k in range(3):
        copy = pltpu.make_async_copy(win_ref.at[k], w.at[k], w_sem.at[k])
        copy.start()
        loads.append(copy)
    own_out = pltpu.make_async_copy(wout_ref, wo.at[pl.ds(0, WIDTH)], w_sem.at[3])
    own_out.start()

    barrier = pltpu.get_barrier_semaphore()
    for step in range(1, 8):
        pl.semaphore_signal(
            barrier, inc=1, device_id=(lax.rem(me + step, 8), row), device_id_type=MESH
        )
    for target in ((me, mate), (other + x, far_row)):
        pl.semaphore_signal(barrier, inc=1, device_id=target, device_id_type=MESH)
    has_outer = jnp.logical_and(outer >= 0, outer < 16)

    @pl.when(has_outer)
    def _():
        pl.semaphore_signal(barrier, inc=1, device_id=(me, outer), device_id_type=MESH)

    shift = shift_ref[0]
    token = lax.broadcasted_iota(jnp.int32, (TOK, TOK), 0)
    source = lax.broadcasted_iota(jnp.int32, (TOK, TOK), 1)
    rows_q, cols_q = packed_place(shift, token)
    pick_fine = one_hot(source == rows_q * 16 + cols_q)
    for c in range(4):
        lanes = slice(c * CHUNK, (c + 1) * CHUNK)
        mixed[:, lanes] = jnp.dot(
            pick_fine, deg_ref[:, lanes], preferred_element_type=F32
        ).astype(BF)

    @pl.when(has_outer)
    def _():
        pl.semaphore_wait(barrier, 10)

    @pl.when(jnp.logical_not(has_outer))
    def _():
        pl.semaphore_wait(barrier, 9)

    def remote(src, dst, send, recv, target):
        copy = pltpu.make_async_remote_copy(
            src_ref=src, dst_ref=dst, send_sem=send, recv_sem=recv,
            device_id=target, device_id_type=MESH,
        )
        copy.start()
        return copy

    base_copies = []
    for step in range(1, 8):
        to = lax.rem(me + step, 8)
        base_copies.append(
            remote(base_ref.at[to], b.at[me], base_sem.at[0, step], base_sem.at[1, step], (to, row))
        )
    own_base = pltpu.make_async_copy(base_ref.at[me], b.at[me], base_sem.at[0, 0])
    own_base.start()

    sends = []

    def item(plane, column):
        return (here if plane == 0 else other) + column

    def x_push(direction, plane, column, t, forward=0):
        frame = item(plane, column)
        to = right if direction == 0 else left
        sends.append(
            remote(g.at[frame, t], g.at[frame, t], x_send.at[direction, plane, forward, t],
                   g_recv.at[frame, t], (here + to, row))
        )

    def z_push(slot, column, t):
        frame = item(0, column)
        sends.append(
            remote(g.at[frame, t], g.at[frame, t], z_send.at[slot, t],
                   g_recv.at[frame, t], (other + x, row))
        )

    def arrive(plane, column, t):
        frame = item(plane, column)
        pltpu.make_async_remote_copy(
            src_ref=g.at[frame, t], dst_ref=g.at[frame, t], send_sem=z_send.at[0, 0],
            recv_sem=g_recv.at[frame, t], device_id=(other + x, row), device_id_type=MESH,
        ).wait_recv()

    def heading(plane, t):
        return (t // 2 + plane) % 2

    own_base.wait()
    for copy in base_copies:
        copy.wait()
    coarse = jnp.concatenate([b[j] for j in range(8)], axis=0)

    def mix(c):
        rows = slice(c * SIDE, (c + 1) * SIDE)
        fine = lax.broadcasted_iota(jnp.int32, (SIDE, QTR), 0) + c * SIDE
        at = lax.broadcasted_iota(jnp.int32, (SIDE, QTR), 1)
        rows_c, cols_c = packed_place(shift, fine)
        pick = one_hot(at == (cols_c // 2) * 4 + rows_c // 2)
        square = jnp.zeros((SIDE, 1), F32)
        for k in range(4):
            lanes = slice(k * CHUNK, (k + 1) * CHUNK)
            up = jnp.dot(pick, coarse[:, lanes], preferred_element_type=F32)
            total = (up + mixed[rows, lanes].astype(F32)).astype(BF)
            mixed[rows, lanes] = total
            total = total.astype(F32)
            square = square + jnp.sum(total * total, axis=1, keepdims=True)
        scale = lax.rsqrt(square * (1.0 / D) + 1e-06)
        for k in range(4):
            lanes = slice(k * CHUNK, (k + 1) * CHUNK)
            normed = mixed[rows, lanes].astype(F32) * scale * gain_ref[:, lanes]
            g[me, 2 * c : 2 * c + 2, :, lanes] = normed.astype(BF).reshape(2, QTR, CHUNK)

    def push_own(c):
        a, l = 2 * c, 2 * c + 1
        z_push(0, x, a)
        x_push(0, 0, x, a)
        x_push(1, 0, x, a)
        x_push(0, 0, x, l)
        x_push(1, 0, x, l)
        z_push(0, x, l)

    def wave_one(c):
        a, l = 2 * c, 2 * c + 1
        arrive(1, x, a)
        x_push(0, 1, x, a)
        x_push(1, 1, x, a)
        for t in (a, l):
            arrive(0, left, t)
            if heading(0, t) == 0:
                x_push(0, 0, left, t, 1)
            if t == l:
                z_push(1, left, t)
            arrive(0, right, t)
            if heading(0, t) == 1:
                x_push(1, 0, right, t, 1)
            if t == l:
                z_push(2, right, t)

    def wave_two(c):
        a, l = 2 * c, 2 * c + 1
        arrive(1, left, a)
        if heading(1, a) == 0:
            x_push(0, 1, left, a, 1)
        arrive(1, right, a)
        if heading(1, a) == 1:
            x_push(1, 1, right, a, 1)
        arrive(0, opp, l)
        z_push(3, opp, l)
        arrive(0, opp, a)

    kv_copies = ([], [])

    def project(c, *pieces):
        frames = [item(plane, column) for plane, column in pieces]
        tokens = jnp.concatenate(
            [g[frame, 2 * c : 2 * c + 2].reshape(SIDE, D) for frame in frames], axis=0
        )
        for k in range(3):
            result = jnp.dot(tokens, w[k], preferred_element_type=F32)
            if k == 0:
                result = result * FACTOR
            result = result.astype(BF)
            for i, frame in enumerate(frames):
                value = result[i * SIDE : (i + 1) * SIDE]
                if k == 0:
                    q[c, frame] = value
                else:
                    kv[1, c, frame, :, (k - 1) * WIDTH : k * WIDTH] = value
        for frame in frames:
            n = len(kv_copies[c])
            up = pltpu.make_async_remote_copy(
                src_ref=kv.at[1, c, frame], dst_ref=kv.at[0, c, frame],
                send_sem=kv_send.at[0, c, n], recv_sem=kv_recv.at[0, c, n],
                device_id=(me, row + 1), device_id_type=MESH,
            )
            down = pltpu.make_async_remote_copy(
                src_ref=kv.at[1, c, frame], dst_ref=kv.at[2, c, frame],
                send_sem=kv_send.at[1, c, n], recv_sem=kv_recv.at[1, c, n],
                device_id=(me, row - 1), device_id_type=MESH,
            )
            kv_copies[c].append((up, down))

            @pl.when(row < 15)
            def _():
                up.start()

            @pl.when(row > 0)
            def _():
                down.start()

    def attend(c):
        @pl.when(row > 0)
        def _():
            for up, down in kv_copies[c]:
                up.wait_recv()

        @pl.when(row < 15)
        def _():
            for up, down in kv_copies[c]:
                down.wait_recv()

        even = (lax.broadcasted_iota(jnp.int32, (SIDE, 2 * WIDTH), 0) // 8) % 2 == 0

        def merge(f, carry):
            kv[3, c, f] = jnp.where(
                even, kv[2, c, f].astype(F32), kv[0, c, f].astype(F32)
            ).astype(BF)
            return carry

        lax.fori_loop(0, 8, merge, 0)
        two = lax.broadcasted_iota(jnp.int32, (TOK, HEAD), 0)
        lane = lax.broadcasted_iota(jnp.int32, (TOK, HEAD), 1)
        query_row = one_hot((two // 8) % 2 == lane)
        ones = jnp.ones((2 * 512, HEAD), BF)

        def block(j, carry):
            at = pl.ds(pl.multiple_of(j * 16, 16), 16)
            own_bias = bias_own[j].reshape(512, HEAD)
            rim_bias = bias_rim[j]
            bias = jnp.concatenate([own_bias, rim_bias], axis=0)
            for h in range(3):
                kl = slice(h * HEAD, (h + 1) * HEAD)
                vl = slice(WIDTH + h * HEAD, WIDTH + (h + 1) * HEAD)
                query = q[c, :, at, kl].reshape(TOK, HEAD)
                keys = [kv[1, c, :, :, kl].reshape(512, HEAD)]
                values = [kv[1, c, :, :, vl].reshape(512, HEAD)]
                for p in range(4):
                    band = jnp.where(j > p, 2, jnp.where(j == p, 3, 0))
                    keys.append(kv[band, c, :, 16 * p : 16 * p + 16, kl].reshape(TOK, HEAD))
                    values.append(kv[band, c, :, 16 * p : 16 * p + 16, vl].reshape(TOK, HEAD))
                key = jnp.concatenate([jnp.concatenate(keys, axis=0), bias], axis=1)
                value = jnp.concatenate([jnp.concatenate(values, axis=0), ones], axis=1)
                scores = lax.dot_general(
                    jnp.concatenate([query, query_row], axis=1), key,
                    (((1,), (1,)), ((), ())), preferred_element_type=F32,
                )
                raised = jnp.exp2(scores - jnp.max(scores, axis=1, keepdims=True))
                result = jnp.dot(raised.astype(BF), value, preferred_element_type=F32)
                result = result[:, :HEAD] / result[:, HEAD:]
                att[c, :, at, kl] = result.astype(BF).reshape(8, 16, HEAD)
            return carry

        lax.fori_loop(0, 4, block, 0)

    order = (opp, right, left, x)
    crossing = ([], [])

    def cross(c):
        for k, column in enumerate(order):
            crossing[c].append(
                remote(att.at[c, other + column], pair.at[c, k], pair_send.at[c, k],
                       pair_recv.at[c, k], (other + x, row))
            )

    def multiply(c, first):
        halves = []
        for k in (first, first + 1):
            crossing[c][k].wait_recv()
            halves.append(jnp.concatenate([att[c, here + order[k]], pair[c, k]], axis=1))
        tokens = jnp.concatenate(halves, axis=0)
        for n in range(4):
            lanes = slice(n * CHUNK, (n + 1) * CHUNK)
            part[c, first : first + 2, :, :, lanes] = (
                jnp.dot(tokens, wo[:, lanes], preferred_element_type=F32)
                .astype(BF)
                .reshape(2, 2, QTR, CHUNK)
            )

    ring = {}

    def push(c, direction, slot, k, h):
        to = right if direction == 0 else left
        ring[c, direction, slot] = remote(
            part.at[c, k, h], inbox.at[c, direction, slot], part_send.at[c, direction, slot],
            part_recv.at[c, direction, slot], (here + to, row),
        )

    def scatter_start(c):
        multiply(c, 0)
        push(c, 0, 0, 0, 0)
        push(c, 1, 0, 0, 1)
        push(c, 0, 1, 1, 1)
        multiply(c, 2)
        push(c, 1, 1, 2, 0)

    def scatter_next(c):
        ring[c, 0, 0].wait_recv()
        part[c, 1, 0] = (part[c, 1, 0].astype(F32) + inbox[c, 0, 0].astype(F32)).astype(BF)
        push(c, 0, 2, 1, 0)
        ring[c, 1, 0].wait_recv()
        part[c, 2, 1] = (part[c, 2, 1].astype(F32) + inbox[c, 1, 0].astype(F32)).astype(BF)
        push(c, 1, 2, 2, 1)

    def scatter_end(c):
        for direction in range(2):
            for slot in (1, 2):
                ring[c, direction, slot].wait_recv()
        for h in range(2):
            rows = slice(c * SIDE + h * QTR, c * SIDE + (h + 1) * QTR)
            total = part[c, 3, h].astype(F32) + inbox[c, 0, 2 - h].astype(F32)
            total = total + inbox[c, 1, 1 + h].astype(F32)
            mixed[rows, :] = (total + mixed[rows, :].astype(F32)).astype(BF)

    mix(0)
    push_own(0)
    mix(1)

    first_row = row * 8
    lane = lax.broadcasted_iota(jnp.int32, (16, HEAD), 1)
    second = lax.broadcasted_iota(jnp.int32, (16, HEAD), 0) // 8

    def number_of(at):
        inside = jnp.logical_and(at >= 0, at < 128)
        return jnp.where(inside, rw_ref[jnp.clip(at, 0, 127)], -1)

    for j in range(4):
        for p in range(4):
            for rim in range(2):
                tile = jnp.zeros((16, HEAD), F32)
                for s in range(2):
                    i = 2 * p + s
                    key_row = first_row + i
                    if rim:
                        key_row = key_row + (8 if i <= 2 * j else -8)
                    key_number = number_of(key_row)
                    for l in range(2):
                        off = key_number != rw_ref[first_row + 2 * j + l]
                        level = jnp.where(off, -1e30, 0.0)
                        tile = jnp.where(
                            jnp.logical_and(lane == l, second == s), level, tile
                        )
                tile = jnp.broadcast_to(tile.astype(BF)[None], (8, 16, HEAD))
                if rim:
                    bias_rim[j, p * TOK : (p + 1) * TOK, :] = tile.reshape(TOK, HEAD)
                else:
                    bias_own[j, :, 16 * p : 16 * p + 16, :] = tile

    own_out.wait()
    half = WIDTH // 2
    core = lax.rem(row, 2)
    mine = wo.at[pl.ds(pl.multiple_of(core * half, half), half)]
    theirs = wo.at[pl.ds(pl.multiple_of(WIDTH + core * half, half), half)]
    wo_first = remote(mine, theirs, wo_sem.at[0], wo_sem.at[1], (other + x, far_row))

    @pl.when(row == 0)
    def _():
        kv[0] = jnp.zeros((2, 8, SIDE, 2 * WIDTH), BF)

    @pl.when(row == 15)
    def _():
        kv[2] = jnp.zeros((2, 8, SIDE, 2 * WIDTH), BF)

    wave_one(0)
    push_own(1)
    for copy in loads:
        copy.wait()
    project(0, (0, x), (0, left))
    wave_two(0)
    project(0, (0, right), (0, opp))
    arrive(1, x, 1)
    arrive(1, left, 1)
    project(0, (1, x), (1, left))
    wave_one(1)
    arrive(1, right, 1)
    arrive(1, opp, 0)
    arrive(1, opp, 1)
    project(0, (1, right), (1, opp))
    wo_first.wait_recv()
    wo_second = remote(theirs, theirs, wo_sem.at[2], wo_sem.at[3], (me, mate))
    project(1, (0, x), (0, left))
    wave_two(1)
    attend(0)
    cross(0)
    project(1, (0, right), (0, opp))
    arrive(1, x, 3)
    arrive(1, left, 3)
    project(1, (1, x), (1, left))
    arrive(1, right, 3)
    arrive(1, opp, 2)
    arrive(1, opp, 3)
    project(1, (1, right), (1, opp))
    wo_second.wait_recv()
    scatter_start(0)
    attend(1)
    cross(1)
    scatter_next(0)
    scatter_start(1)
    scatter_end(0)
    scatter_next(1)
    scatter_end(1)

    rows_p, cols_p = packed_place(shift, source)
    unpick = one_hot(token == rows_p * 16 + cols_p)
    for c in range(4):
        lanes = slice(c * CHUNK, (c + 1) * CHUNK)
        out_ref[:, lanes] = jnp.dot(
            unpick, mixed[:, lanes], preferred_element_type=F32
        ).astype(BF)

    for copy in sends:
        copy.wait_send()
    wo_first.wait_send()
    wo_second.wait_send()
    for c in range(2):
        for copy in crossing[c]:
            copy.wait_send()
        for direction in range(2):
            for slot in range(3):
                ring[c, direction, slot].wait_send()

    @pl.when(row < 15)
    def _():
        for c in range(2):
            for up, down in kv_copies[c]:
                up.wait_send()

    @pl.when(row > 0)
    def _():
        for c in range(2):
            for up, down in kv_copies[c]:
                down.wait_send()


VM = pl.BlockSpec(memory_space=pltpu.VMEM)
SM = pl.BlockSpec(memory_space=pltpu.SMEM)
ANY = pl.BlockSpec(memory_space=pl.ANY)
DMA = pltpu.SemaphoreType.DMA


def local(base_latent, degraded, row_window, column_shift, norm_gain, project_in, project_out):
    out = pl.pallas_call(
        layer_kernel,
        out_shape=jax.ShapeDtypeStruct((TOK, D), BF),
        in_specs=[VM, VM, SM, SM, VM, ANY, ANY],
        out_specs=VM,
        scratch_shapes=[
            pltpu.VMEM((8, 4, QTR, D), BF),
            pltpu.VMEM((8, 4, D), BF),
            pltpu.VMEM((3, D, WIDTH), BF),
            pltpu.VMEM((2 * WIDTH, D), BF),
            pltpu.VMEM((TOK, D), BF),
            pltpu.VMEM((2, 8, SIDE, WIDTH), BF),
            pltpu.VMEM((4, 2, 8, SIDE, 2 * WIDTH), BF),
            pltpu.VMEM((2, 8, SIDE, WIDTH), BF),
            pltpu.VMEM((2, 4, SIDE, WIDTH), BF),
            pltpu.VMEM((2, 4, 2, QTR, D), BF),
            pltpu.VMEM((2, 2, 3, QTR, D), BF),
            pltpu.VMEM((4, 8, SIDE, HEAD), BF),
            pltpu.VMEM((4, 4 * TOK, HEAD), BF),
            DMA((2, 8)),
            DMA((2, 2, 2, 4)),
            DMA((4, 4)),
            DMA((8, 4)),
            DMA((2, 2, 8)),
            DMA((2, 2, 8)),
            DMA((4,)),
            DMA((4,)),
            DMA((2, 4)),
            DMA((2, 4)),
            DMA((2, 2, 3)),
            DMA((2, 2, 3)),
        ],
        compiler_params=pltpu.CompilerParams(
            collective_id=0, has_side_effects=True, vmem_limit_bytes=60 * 2**20
        ),
        name="layer",
    )(
        base_latent.reshape(8, 4, D),
        degraded.reshape(TOK, D),
        column_shift,
        row_window,
        norm_gain.reshape(1, D),
        project_in.transpose(1, 0, 2),
        project_out,
    )
    return out.reshape(1, 8, 16, D)


def solution(mesh):
    placed = (
        P(None, "row", "frame", None),
        P("frame", "row", None, None),
        P(),
        P(),
        P(),
        P(None, None, "frame"),
        P("frame", None),
    )
    return jax.shard_map(
        local, mesh=mesh, in_specs=placed, out_specs=P("frame", "row", None, None), check_vma=False
    )
```

time: 414 us -> 107 us (0.26)
  waiting for transfers between devices: 272 us -> 0 us
  Pallas kernels: 0 us -> 104 us
  matrix products: 54.3 us -> 0 us
  local copies, waits for them, and re-layouts: 31.1 us -> 2.06 us
  blocking collectives: 18 us -> 0 us
  other arithmetic: 16.1 us -> 0 us
  between operations: 14.3 us -> 0.66 us
  starting transfers between devices: 6.92 us -> 0 us
    all_gather x1 -> x0, waiting for transfers between devices: 191 us -> none  [local(): piece = lax.all_gather(rim_tokens, 'frame', axis=0, tiled=True)]
    pallas_call x0 -> x1, Pallas kernels: none -> 104 us  [local(): pl.pallas_call(layer_kernel, out_shape=jax.ShapeDtypeStruct((TOK, D), BF)...]
    reduce_scatter x1 -> x0, waiting for transfers between devices: 71.9 us -> none  [local(): lax.psum_scatter(jnp.einsum('frck,ke->frce', attended, project_out, prefe...]
    dot_general x15 -> x0, matrix products: 54.3 us -> none  [the longest x1 19.3 us: local(): jnp.einsum('frcd,dkh->frckh', piece, pair_weight, preferred_element_type=...]
    all_to_all x1 -> x0, blocking collectives: 18 us -> none  [local(): lax.all_to_all(fine_tokens, 'frame', split_axis=0, concat_axis=2, tiled=T...]
    reshape x3 -> x0, local copies, waits for them, and re-layouts: 13.5 us -> none  [the longest x1 12.9 us: window_attention(): keyval.reshape(frame_count, key_rows, windows, WIN_COLS, 2, head_count, H...]
    slice x3 -> x0, local copies, waits for them, and re-layouts: 9.2 us -> none  [window_attention(): results = lax.map(one_block, (query_blocks, pair_blocks[0], pair_blocks[1]))]
    ppermute x2 -> x0, waiting for transfers between devices: 8.91 us -> none  [the longest x1 7.73 us: extended(): lax.ppermute(lax.slice_in_dim(block, 0, width, axis=dim), axis, backward)]
  transfers between devices with their start and end apart: 4 -> 0, of which waited for: 4 -> 0; matrix products, arithmetic and copies ran while one was open for 0% -> 0% of each run, Pallas kernels for 0% -> 0%
where the time goes in v2:
time: 107 us; the launch traced here: 106 us
  Pallas kernels  104 us (97%)
  local copies, waits for them, and re-layouts  2.06 us (2%)
    pallas_call x1, Pallas kernels, local(): pl.pallas_call(layer_kernel, out_shape=jax.ShapeDtypeStruct((TOK, D), BF)...  104 us

profile of v2, /device:TPU:1, one launch (start us, length us, event | category | flops | bytes accessed | tf_op | source)
XLA Modules:
  0.0 106.5 jit_solution(2301741432431085001)
XLA Ops:
  0.7 103.8 %layer.1 = bf16[128,3072]{1,0:T(8,128)(2,1)} custom-call(bf16[8,4,3072]{2,1,0:T(4,128)(2,1)} %bitcast.8, bf16[128,3072]{1,0:T(8,128)(2,1)} %bitcast.7, s32[1]{0:T(128)S(6)} %copy.9.shift_ref, s32[128]{0:T(128)} %rw_ref.1, f32[1,3072]{1,0:T(1,128)} %bitcast.9, bf16[3,3072,384]{2,1,0:T(8,128)(2,1)} %bitcast.5, bf16[384,3072]{1,0:T(8,128)(2,1)} %wout_ref.1), custom_call_target="tpu_custom_call" | custom-call | tf_op jit(solution)/shard_map/layer/pallas_call | solution.py:477
  104.4 2.1 %copy.10 = bf16[1,8,16,3072]{3,2,1,0:T(8,128)(2,1)} copy(bf16[1,8,16,3072]{3,2,1,0:T(8,128)(2,1)} %bitcast.6) | data formatting | bytes 1572864

commit v3 on v2

--- a/solution.py
+++ b/solution.py
@@ -15,6 +15,14 @@
 CHUNK = 768
 BF = jnp.bfloat16
 F32 = jnp.float32
+PIECE = 16
+FIRST = ((0, 1, 2), (4, 5, 6))
+LATE = ((3,), (7,))
+HEADING = {}
+for PIECES in zip(FIRST, LATE):
+    for GROUP, PLANE in ((0, 1), (0, 0), (1, 0)):
+        for T in PIECES[GROUP]:
+            HEADING[PLANE, T] = len(HEADING) % 2
 FACTOR = HEAD ** (-0.5) * 1.4426950408889634
 
 
@@ -31,7 +39,7 @@
 def layer_kernel(
     base_ref, deg_ref, shift_ref, rw_ref, gain_ref, win_ref, wout_ref,
     out_ref,
-    g, b, w, wo, mixed, q, kv, att, pair, part, inbox, bias_own, bias_rim,
+    deg, g, b, w, wo, mixed, q, kv, att, pair, part, inbox, bias,
     base_sem, x_send, z_send, g_recv, kv_send, kv_recv, w_sem, wo_sem,
     pair_send, pair_recv, part_send, part_recv,
 ):
@@ -44,6 +52,21 @@
     outer = row + 2 * lax.rem(row, 2) - 1
     far_row = lax.rem(row + 8, 16)
 
+    barrier = pltpu.get_barrier_semaphore()
+    for step in range(1, 8):
+        pl.semaphore_signal(
+            barrier, inc=1, device_id=(lax.rem(me + step, 8), row), device_id_type=MESH
+        )
+    for target in ((me, mate), (other + x, far_row)):
+        pl.semaphore_signal(barrier, inc=1, device_id=target, device_id_type=MESH)
+    has_outer = jnp.logical_and(outer >= 0, outer < 16)
+
+    @pl.when(has_outer)
+    def _():
+        pl.semaphore_signal(barrier, inc=1, device_id=(me, outer), device_id_type=MESH)
+
+    deg_load = pltpu.make_async_copy(deg_ref, deg, w_sem.at[4])
+    deg_load.start()
     loads = []
     for k in range(3):
         copy = pltpu.make_async_copy(win_ref.at[k], w.at[k], w_sem.at[k])
@@ -52,28 +75,16 @@
     own_out = pltpu.make_async_copy(wout_ref, wo.at[pl.ds(0, WIDTH)], w_sem.at[3])
     own_out.start()
 
-    barrier = pltpu.get_barrier_semaphore()
-    for step in range(1, 8):
-        pl.semaphore_signal(
-            barrier, inc=1, device_id=(lax.rem(me + step, 8), row), device_id_type=MESH
-        )
-    for target in ((me, mate), (other + x, far_row)):
-        pl.semaphore_signal(barrier, inc=1, device_id=target, device_id_type=MESH)
-    has_outer = jnp.logical_and(outer >= 0, outer < 16)
-
-    @pl.when(has_outer)
-    def _():
-        pl.semaphore_signal(barrier, inc=1, device_id=(me, outer), device_id_type=MESH)
-
     shift = shift_ref[0]
     token = lax.broadcasted_iota(jnp.int32, (TOK, TOK), 0)
     source = lax.broadcasted_iota(jnp.int32, (TOK, TOK), 1)
     rows_q, cols_q = packed_place(shift, token)
     pick_fine = one_hot(source == rows_q * 16 + cols_q)
+    deg_load.wait()
     for c in range(4):
         lanes = slice(c * CHUNK, (c + 1) * CHUNK)
         mixed[:, lanes] = jnp.dot(
-            pick_fine, deg_ref[:, lanes], preferred_element_type=F32
+            pick_fine, deg[:, lanes], preferred_element_type=F32
         ).astype(BF)
 
     @pl.when(has_outer)
@@ -127,9 +138,6 @@
             src_ref=g.at[frame, t], dst_ref=g.at[frame, t], send_sem=z_send.at[0, 0],
             recv_sem=g_recv.at[frame, t], device_id=(other + x, row), device_id_type=MESH,
         ).wait_recv()
-
-    def heading(plane, t):
-        return (t // 2 + plane) % 2
 
     own_base.wait()
     for copy in base_copies:
@@ -154,52 +162,65 @@
         for k in range(4):
             lanes = slice(k * CHUNK, (k + 1) * CHUNK)
             normed = mixed[rows, lanes].astype(F32) * scale * gain_ref[:, lanes]
-            g[me, 2 * c : 2 * c + 2, :, lanes] = normed.astype(BF).reshape(2, QTR, CHUNK)
+            g[me, 4 * c : 4 * c + 4, :, lanes] = normed.astype(BF).reshape(4, PIECE, CHUNK)
 
     def push_own(c):
-        a, l = 2 * c, 2 * c + 1
-        z_push(0, x, a)
-        x_push(0, 0, x, a)
-        x_push(1, 0, x, a)
-        x_push(0, 0, x, l)
-        x_push(1, 0, x, l)
-        z_push(0, x, l)
+        for t in FIRST[c]:
+            z_push(0, x, t)
+        for t in FIRST[c] + LATE[c]:
+            x_push(0, 0, x, t)
+            x_push(1, 0, x, t)
+        for t in LATE[c]:
+            z_push(0, x, t)
 
     def wave_one(c):
-        a, l = 2 * c, 2 * c + 1
-        arrive(1, x, a)
-        x_push(0, 1, x, a)
-        x_push(1, 1, x, a)
-        for t in (a, l):
+        for t in FIRST[c]:
+            arrive(1, x, t)
+            x_push(0, 1, x, t)
+            x_push(1, 1, x, t)
+        for t in FIRST[c] + LATE[c]:
             arrive(0, left, t)
-            if heading(0, t) == 0:
+            if HEADING[0, t] == 0:
                 x_push(0, 0, left, t, 1)
-            if t == l:
+            if t in LATE[c]:
                 z_push(1, left, t)
             arrive(0, right, t)
-            if heading(0, t) == 1:
+            if HEADING[0, t] == 1:
                 x_push(1, 0, right, t, 1)
-            if t == l:
+            if t in LATE[c]:
                 z_push(2, right, t)
 
     def wave_two(c):
-        a, l = 2 * c, 2 * c + 1
-        arrive(1, left, a)
-        if heading(1, a) == 0:
-            x_push(0, 1, left, a, 1)
-        arrive(1, right, a)
-        if heading(1, a) == 1:
-            x_push(1, 1, right, a, 1)
-        arrive(0, opp, l)
-        z_push(3, opp, l)
-        arrive(0, opp, a)
+        for t in FIRST[c]:
+            arrive(1, left, t)
+            if HEADING[1, t] == 0:
+                x_push(0, 1, left, t, 1)
+            arrive(1, right, t)
+            if HEADING[1, t] == 1:
+                x_push(1, 1, right, t, 1)
+        for t in LATE[c]:
+            arrive(0, opp, t)
+            z_push(3, opp, t)
+        for t in FIRST[c]:
+            arrive(0, opp, t)
+
+    def wave_three(c):
+        for column in (x, left):
+            for t in LATE[c]:
+                arrive(1, column, t)
+
+    def wave_four(c):
+        for t in LATE[c]:
+            arrive(1, right, t)
+        for t in FIRST[c] + LATE[c]:
+            arrive(1, opp, t)
 
     kv_copies = ([], [])
 
     def project(c, *pieces):
         frames = [item(plane, column) for plane, column in pieces]
         tokens = jnp.concatenate(
-            [g[frame, 2 * c : 2 * c + 2].reshape(SIDE, D) for frame in frames], axis=0
+            [g[frame, 4 * c : 4 * c + 4].reshape(SIDE, D) for frame in frames], axis=0
         )
         for k in range(3):
             result = jnp.dot(tokens, w[k], preferred_element_type=F32)
@@ -254,55 +275,51 @@
             return carry
 
         lax.fori_loop(0, 8, merge, 0)
-        two = lax.broadcasted_iota(jnp.int32, (TOK, HEAD), 0)
-        lane = lax.broadcasted_iota(jnp.int32, (TOK, HEAD), 1)
-        query_row = one_hot((two // 8) % 2 == lane)
         ones = jnp.ones((2 * 512, HEAD), BF)
 
-        def block(j, carry):
-            at = pl.ds(pl.multiple_of(j * 16, 16), 16)
-            own_bias = bias_own[j].reshape(512, HEAD)
-            rim_bias = bias_rim[j]
-            bias = jnp.concatenate([own_bias, rim_bias], axis=0)
-            for h in range(3):
-                kl = slice(h * HEAD, (h + 1) * HEAD)
-                vl = slice(WIDTH + h * HEAD, WIDTH + (h + 1) * HEAD)
-                query = q[c, :, at, kl].reshape(TOK, HEAD)
-                keys = [kv[1, c, :, :, kl].reshape(512, HEAD)]
-                values = [kv[1, c, :, :, vl].reshape(512, HEAD)]
+        def head(h, carry):
+            kl = pl.ds(pl.multiple_of(h * HEAD, HEAD), HEAD)
+            vl = pl.ds(pl.multiple_of(WIDTH + h * HEAD, HEAD), HEAD)
+            own_key = kv[1, c, :, :, kl].reshape(512, HEAD)
+            own_value = kv[1, c, :, :, vl].reshape(512, HEAD)
+            for j in range(4):
+                at = slice(16 * j, 16 * j + 16)
+                keys, values = [own_key], [own_value]
                 for p in range(4):
-                    band = jnp.where(j > p, 2, jnp.where(j == p, 3, 0))
-                    keys.append(kv[band, c, :, 16 * p : 16 * p + 16, kl].reshape(TOK, HEAD))
-                    values.append(kv[band, c, :, 16 * p : 16 * p + 16, vl].reshape(TOK, HEAD))
-                key = jnp.concatenate([jnp.concatenate(keys, axis=0), bias], axis=1)
+                    band = 2 if j > p else (3 if j == p else 0)
+                    rows = slice(16 * p, 16 * p + 16)
+                    keys.append(kv[band, c, :, rows, kl].reshape(TOK, HEAD))
+                    values.append(kv[band, c, :, rows, vl].reshape(TOK, HEAD))
                 value = jnp.concatenate([jnp.concatenate(values, axis=0), ones], axis=1)
                 scores = lax.dot_general(
-                    jnp.concatenate([query, query_row], axis=1), key,
+                    q[c, :, at, kl].reshape(TOK, HEAD), jnp.concatenate(keys, axis=0),
                     (((1,), (1,)), ((), ())), preferred_element_type=F32,
                 )
+                scores = (scores.reshape(8, 16, 2 * 512) + bias[j][None]).reshape(TOK, 2 * 512)
                 raised = jnp.exp2(scores - jnp.max(scores, axis=1, keepdims=True))
                 result = jnp.dot(raised.astype(BF), value, preferred_element_type=F32)
                 result = result[:, :HEAD] / result[:, HEAD:]
-                att[c, :, at, kl] = result.astype(BF).reshape(8, 16, HEAD)
+                att[c, h, :, at, :] = result.astype(BF).reshape(8, 16, HEAD)
+            cross(c, h).start()
             return carry
 
-        lax.fori_loop(0, 4, block, 0)
+        lax.fori_loop(0, 3, head, 0)
+
+    def cross(c, h):
+        return pltpu.make_async_remote_copy(
+            src_ref=att.at[c, h, pl.ds(other, 4)], dst_ref=pair.at[c, h],
+            send_sem=pair_send.at[c, h], recv_sem=pair_recv.at[c, h],
+            device_id=(other + x, row), device_id_type=MESH,
+        )
 
     order = (opp, right, left, x)
-    crossing = ([], [])
-
-    def cross(c):
-        for k, column in enumerate(order):
-            crossing[c].append(
-                remote(att.at[c, other + column], pair.at[c, k], pair_send.at[c, k],
-                       pair_recv.at[c, k], (other + x, row))
-            )
 
     def multiply(c, first):
         halves = []
         for k in (first, first + 1):
-            crossing[c][k].wait_recv()
-            halves.append(jnp.concatenate([att[c, here + order[k]], pair[c, k]], axis=1))
+            heads = [att[c, h, here + order[k]] for h in range(3)]
+            heads += [pair[c, h, order[k]] for h in range(3)]
+            halves.append(jnp.concatenate(heads, axis=1))
         tokens = jnp.concatenate(halves, axis=0)
         for n in range(4):
             lanes = slice(n * CHUNK, (n + 1) * CHUNK)
@@ -322,6 +339,8 @@
         )
 
     def scatter_start(c):
+        for h in range(3):
+            cross(c, h).wait_recv()
         multiply(c, 0)
         push(c, 0, 0, 0, 0)
         push(c, 1, 0, 0, 1)
@@ -345,41 +364,33 @@
             rows = slice(c * SIDE + h * QTR, c * SIDE + (h + 1) * QTR)
             total = part[c, 3, h].astype(F32) + inbox[c, 0, 2 - h].astype(F32)
             total = total + inbox[c, 1, 1 + h].astype(F32)
-            mixed[rows, :] = (total + mixed[rows, :].astype(F32)).astype(BF)
+            out_ref[rows, :] = (total + mixed[rows, :].astype(F32)).astype(BF)
 
     mix(0)
     push_own(0)
     mix(1)
 
     first_row = row * 8
-    lane = lax.broadcasted_iota(jnp.int32, (16, HEAD), 1)
-    second = lax.broadcasted_iota(jnp.int32, (16, HEAD), 0) // 8
+    spot = lax.broadcasted_iota(jnp.int32, (16, 2 * 512), 1)
+    second = lax.broadcasted_iota(jnp.int32, (16, 2 * 512), 0) // 8
+    key_row = jnp.where(
+        spot < 512, (spot % SIDE) // 8, 8 + 2 * ((spot - 512) // TOK) + (spot // 8) % 2
+    )
 
     def number_of(at):
         inside = jnp.logical_and(at >= 0, at < 128)
         return jnp.where(inside, rw_ref[jnp.clip(at, 0, 127)], -1)
 
     for j in range(4):
-        for p in range(4):
-            for rim in range(2):
-                tile = jnp.zeros((16, HEAD), F32)
-                for s in range(2):
-                    i = 2 * p + s
-                    key_row = first_row + i
-                    if rim:
-                        key_row = key_row + (8 if i <= 2 * j else -8)
-                    key_number = number_of(key_row)
-                    for l in range(2):
-                        off = key_number != rw_ref[first_row + 2 * j + l]
-                        level = jnp.where(off, -1e30, 0.0)
-                        tile = jnp.where(
-                            jnp.logical_and(lane == l, second == s), level, tile
-                        )
-                tile = jnp.broadcast_to(tile.astype(BF)[None], (8, 16, HEAD))
-                if rim:
-                    bias_rim[j, p * TOK : (p + 1) * TOK, :] = tile.reshape(TOK, HEAD)
-                else:
-                    bias_own[j, :, 16 * p : 16 * p + 16, :] = tile
+        query_number = jnp.where(
+            second == 0, rw_ref[first_row + 2 * j], rw_ref[first_row + 2 * j + 1]
+        )
+        key_number = jnp.zeros((16, 2 * 512), jnp.int32)
+        for i in range(8):
+            key_number = jnp.where(key_row == i, rw_ref[first_row + i], key_number)
+            rim = number_of(first_row + i + (8 if i <= 2 * j else -8))
+            key_number = jnp.where(key_row == 8 + i, rim, key_number)
+        bias[j] = jnp.where(key_number == query_number, 0.0, -1e30)
 
     own_out.wait()
     half = WIDTH // 2
@@ -403,53 +414,36 @@
     project(0, (0, x), (0, left))
     wave_two(0)
     project(0, (0, right), (0, opp))
-    arrive(1, x, 1)
-    arrive(1, left, 1)
+    wave_three(0)
     project(0, (1, x), (1, left))
     wave_one(1)
-    arrive(1, right, 1)
-    arrive(1, opp, 0)
-    arrive(1, opp, 1)
+    wave_four(0)
     project(0, (1, right), (1, opp))
     wo_first.wait_recv()
     wo_second = remote(theirs, theirs, wo_sem.at[2], wo_sem.at[3], (me, mate))
     project(1, (0, x), (0, left))
     wave_two(1)
     attend(0)
-    cross(0)
     project(1, (0, right), (0, opp))
-    arrive(1, x, 3)
-    arrive(1, left, 3)
+    wave_three(1)
     project(1, (1, x), (1, left))
-    arrive(1, right, 3)
-    arrive(1, opp, 2)
-    arrive(1, opp, 3)
+    wave_four(1)
     project(1, (1, right), (1, opp))
     wo_second.wait_recv()
     scatter_start(0)
     attend(1)
-    cross(1)
     scatter_next(0)
     scatter_start(1)
     scatter_end(0)
     scatter_next(1)
     scatter_end(1)
-
-    rows_p, cols_p = packed_place(shift, source)
-    unpick = one_hot(token == rows_p * 16 + cols_p)
-    for c in range(4):
-        lanes = slice(c * CHUNK, (c + 1) * CHUNK)
-        out_ref[:, lanes] = jnp.dot(
-            unpick, mixed[:, lanes], preferred_element_type=F32
-        ).astype(BF)
-
     for copy in sends:
         copy.wait_send()
     wo_first.wait_send()
     wo_second.wait_send()
     for c in range(2):
-        for copy in crossing[c]:
-            copy.wait_send()
+        for h in range(3):
+            cross(c, h).wait_send()
         for direction in range(2):
             for slot in range(3):
                 ring[c, direction, slot].wait_send()
@@ -465,6 +459,13 @@
         for c in range(2):
             for up, down in kv_copies[c]:
                 down.wait_send()
+
+
+def unpack_kernel(shift_ref, packed_ref, out_ref):
+    packed = lax.broadcasted_iota(jnp.int32, (TOK, TOK), 1)
+    rows_p, cols_p = packed_place(shift_ref[0], packed)
+    pick = one_hot(lax.broadcasted_iota(jnp.int32, (TOK, TOK), 0) == rows_p * 16 + cols_p)
+    out_ref[...] = jnp.dot(pick, packed_ref[...], preferred_element_type=F32).astype(BF)
 
 
 VM = pl.BlockSpec(memory_space=pltpu.VMEM)
@@ -477,32 +478,32 @@
     out = pl.pallas_call(
         layer_kernel,
         out_shape=jax.ShapeDtypeStruct((TOK, D), BF),
-        in_specs=[VM, VM, SM, SM, VM, ANY, ANY],
+        in_specs=[ANY, ANY, SM, SM, VM, ANY, ANY],
         out_specs=VM,
         scratch_shapes=[
-            pltpu.VMEM((8, 4, QTR, D), BF),
+            pltpu.VMEM((TOK, D), BF),
+            pltpu.VMEM((8, 8, PIECE, D), BF),
             pltpu.VMEM((8, 4, D), BF),
             pltpu.VMEM((3, D, WIDTH), BF),
             pltpu.VMEM((2 * WIDTH, D), BF),
             pltpu.VMEM((TOK, D), BF),
             pltpu.VMEM((2, 8, SIDE, WIDTH), BF),
             pltpu.VMEM((4, 2, 8, SIDE, 2 * WIDTH), BF),
-            pltpu.VMEM((2, 8, SIDE, WIDTH), BF),
-            pltpu.VMEM((2, 4, SIDE, WIDTH), BF),
+            pltpu.VMEM((2, 3, 8, SIDE, HEAD), BF),
+            pltpu.VMEM((2, 3, 4, SIDE, HEAD), BF),
             pltpu.VMEM((2, 4, 2, QTR, D), BF),
             pltpu.VMEM((2, 2, 3, QTR, D), BF),
-            pltpu.VMEM((4, 8, SIDE, HEAD), BF),
-            pltpu.VMEM((4, 4 * TOK, HEAD), BF),
+            pltpu.VMEM((4, 16, 2 * 512), F32),
             DMA((2, 8)),
-            DMA((2, 2, 2, 4)),
-            DMA((4, 4)),
-            DMA((8, 4)),
+            DMA((2, 2, 2, 8)),
+            DMA((4, 8)),
+            DMA((8, 8)),
             DMA((2, 2, 8)),
             DMA((2, 2, 8)),
+            DMA((5,)),
             DMA((4,)),
-            DMA((4,)),
-            DMA((2, 4)),
-            DMA((2, 4)),
+            DMA((2, 3)),
+            DMA((2, 3)),
             DMA((2, 2, 3)),
             DMA((2, 2, 3)),
         ],
@@ -519,6 +520,13 @@
         project_in.transpose(1, 0, 2),
         project_out,
     )
+    out = pl.pallas_call(
+        unpack_kernel,
+        out_shape=jax.ShapeDtypeStruct((TOK, D), BF),
+        in_specs=[SM, VM],
+        out_specs=VM,
+        name="unpack",
+    )(column_shift, out)
     return out.reshape(1, 8, 16, D)
 
 

time: 107 us -> 99.7 us (0.932)
  Pallas kernels: 104 us -> 98.4 us
  local copies, waits for them, and re-layouts: 2.06 us -> 0 us
    pallas_call x1, Pallas kernels: 104 us -> 96.1 us  [local(): pl.pallas_call(layer_kernel, out_shape=jax.ShapeDtypeStruct((TOK, D), BF)...]
    pallas_call x0 -> x1, Pallas kernels: none -> 2.37 us  [local(): pl.pallas_call(unpack_kernel, out_shape=jax.ShapeDtypeStruct((TOK, D), BF...]
    unnamed x1 -> x0, local copies, waits for them, and re-layouts: 2.06 us -> none
where the time goes in v3:
time: 99.7 us; the launch traced here: 99.1 us
  Pallas kernels  98.4 us (99%)
    pallas_call x1, Pallas kernels, local(): pl.pallas_call(layer_kernel, out_shape=jax.ShapeDtypeStruct((TOK, D), BF)...  96.1 us
    pallas_call x1, Pallas kernels, local(): pl.pallas_call(unpack_kernel, out_shape=jax.ShapeDtypeStruct((TOK, D), BF...  2.37 us

profile of v3, /device:TPU:1, one launch (start us, length us, event | category | flops | bytes accessed | tf_op | source)
XLA Modules:
  0.0 99.1 jit_solution(8312532580557737493)
XLA Ops:
  0.7 96.1 %layer.1.packed_ref = bf16[128,3072]{1,0:T(8,128)(2,1)} custom-call(bf16[8,4,3072]{2,1,0:T(4,128)(2,1)} %bitcast.7, bf16[128,3072]{1,0:T(8,128)(2,1)} %bitcast.6, s32[1]{0:T(128)S(6)} %copy.8.shift_ref, s32[128]{0:T(128)} %rw_ref.1, f32[1,3072]{1,0:T(1,128)} %bitcast.8, bf16[3,3072,384]{2,1,0:T(8,128)(2,1)} %bitcast.5, bf16[384,3072]{1,0:T(8,128)(2,1)} %wout_ref.1), custom_call_target="tpu_custom_call" | custom-call | tf_op jit(solution)/shard_map/layer/pallas_call | solution.py:478
  96.7 2.4 %unpack.1 = bf16[128,3072]{1,0:T(8,128)(2,1)} custom-call(s32[1]{0:T(128)S(6)} %copy.8.shift_ref, bf16[128,3072]{1,0:T(8,128)(2,1)} %layer.1.packed_ref), custom_call_target="tpu_custom_call" | custom-call | tf_op jit(solution)/shard_map/unpack/pallas_call | solution.py:523

commit v4 on v3

--- a/solution.py
+++ b/solution.py
@@ -167,7 +167,7 @@
     def push_own(c):
         for t in FIRST[c]:
             z_push(0, x, t)
-        for t in FIRST[c] + LATE[c]:
+        for t in LATE[c] + FIRST[c]:
             x_push(0, 0, x, t)
             x_push(1, 0, x, t)
         for t in LATE[c]:
@@ -178,7 +178,7 @@
             arrive(1, x, t)
             x_push(0, 1, x, t)
             x_push(1, 1, x, t)
-        for t in FIRST[c] + LATE[c]:
+        for t in LATE[c] + FIRST[c]:
             arrive(0, left, t)
             if HEADING[0, t] == 0:
                 x_push(0, 0, left, t, 1)
@@ -408,11 +408,11 @@
         kv[2] = jnp.zeros((2, 8, SIDE, 2 * WIDTH), BF)
 
     wave_one(0)
-    push_own(1)
     for copy in loads:
         copy.wait()
     project(0, (0, x), (0, left))
     wave_two(0)
+    push_own(1)
     project(0, (0, right), (0, opp))
     wave_three(0)
     project(0, (1, x), (1, left))

time: 99.7 us -> 98.8 us (level)
  Pallas kernels: 98.4 us -> 97.2 us
    pallas_call x1, Pallas kernels: 96.1 us -> 94.8 us  [local(): pl.pallas_call(layer_kernel, out_shape=jax.ShapeDtypeStruct((TOK, D), BF)...]
where the time goes in v4:
time: 98.8 us; the launch traced here: 97.8 us
  Pallas kernels  97.2 us (98%)
    pallas_call x1, Pallas kernels, local(): pl.pallas_call(layer_kernel, out_shape=jax.ShapeDtypeStruct((TOK, D), BF)...  94.8 us
    pallas_call x1, Pallas kernels, local(): pl.pallas_call(unpack_kernel, out_shape=jax.ShapeDtypeStruct((TOK, D), BF...  2.37 us

profile of v4, /device:TPU:1, one launch (start us, length us, event | category | flops | bytes accessed | tf_op | source)
XLA Modules:
  0.0 97.8 jit_solution(5667084028965478879)
XLA Ops:
  0.7 94.8 %layer.1.packed_ref = bf16[128,3072]{1,0:T(8,128)(2,1)} custom-call(bf16[8,4,3072]{2,1,0:T(4,128)(2,1)} %bitcast.7, bf16[128,3072]{1,0:T(8,128)(2,1)} %bitcast.6, s32[1]{0:T(128)S(6)} %copy.8.shift_ref, s32[128]{0:T(128)} %rw_ref.1, f32[1,3072]{1,0:T(1,128)} %bitcast.8, bf16[3,3072,384]{2,1,0:T(8,128)(2,1)} %bitcast.5, bf16[384,3072]{1,0:T(8,128)(2,1)} %wout_ref.1), custom_call_target="tpu_custom_call" | custom-call | tf_op jit(solution)/shard_map/layer/pallas_call | solution.py:478
  95.5 2.4 %unpack.1 = bf16[128,3072]{1,0:T(8,128)(2,1)} custom-call(s32[1]{0:T(128)S(6)} %copy.8.shift_ref, bf16[128,3072]{1,0:T(8,128)(2,1)} %layer.1.packed_ref), custom_call_target="tpu_custom_call" | custom-call | tf_op jit(solution)/shard_map/unpack/pallas_call | solution.py:523

commit v5 on v4

--- a/solution.py
+++ b/solution.py
@@ -412,8 +412,8 @@
         copy.wait()
     project(0, (0, x), (0, left))
     wave_two(0)
+    project(0, (0, right), (0, opp))
     push_own(1)
-    project(0, (0, right), (0, opp))
     wave_three(0)
     project(0, (1, x), (1, left))
     wave_one(1)

time: 98.8 us -> 98.8 us (level)
  no operation moved by 1% of the time
where the time goes in v5:
time: 98.8 us; the launch traced here: 97.8 us
  Pallas kernels  97.2 us (98%)
    pallas_call x1, Pallas kernels, local(): pl.pallas_call(layer_kernel, out_shape=jax.ShapeDtypeStruct((TOK, D), BF)...  94.8 us
    pallas_call x1, Pallas kernels, local(): pl.pallas_call(unpack_kernel, out_shape=jax.ShapeDtypeStruct((TOK, D), BF...  2.37 us

profile of v5, /device:TPU:1, one launch (start us, length us, event | category | flops | bytes accessed | tf_op | source)
XLA Modules:
  0.0 97.8 jit_solution(15515111270655869316)
XLA Ops:
  0.7 94.8 %layer.1.packed_ref = bf16[128,3072]{1,0:T(8,128)(2,1)} custom-call(bf16[8,4,3072]{2,1,0:T(4,128)(2,1)} %bitcast.7, bf16[128,3072]{1,0:T(8,128)(2,1)} %bitcast.6, s32[1]{0:T(128)S(6)} %copy.8.shift_ref, s32[128]{0:T(128)} %rw_ref.1, f32[1,3072]{1,0:T(1,128)} %bitcast.8, bf16[3,3072,384]{2,1,0:T(8,128)(2,1)} %bitcast.5, bf16[384,3072]{1,0:T(8,128)(2,1)} %wout_ref.1), custom_call_target="tpu_custom_call" | custom-call | tf_op jit(solution)/shard_map/layer/pallas_call | solution.py:478
  95.5 2.4 %unpack.1 = bf16[128,3072]{1,0:T(8,128)(2,1)} custom-call(s32[1]{0:T(128)S(6)} %copy.8.shift_ref, bf16[128,3072]{1,0:T(8,128)(2,1)} %layer.1.packed_ref), custom_call_target="tpu_custom_call" | custom-call | tf_op jit(solution)/shard_map/unpack/pallas_call | solution.py:523
